TPU v7x, 32 devices: a whole 2x2x4 slice. The times are simulated.
32 devices in a mesh: rows: 8 (over z, y), rhs: 4 (over x, core).
Axes of the slice: x: 2, y: 2, z: 4, core: 2. Of those that a mesh axis runs over, the one named last changes fastest.
Arguments:
- kernel_rows: bfloat16 [16384, 512], P(('rows', 'rhs')), may hold values from 0 to 1
- factor_blocks: bfloat16 [64, 8, 256, 256], P('rows'), may hold values from -0.125 to 0.125
- diag_inverse: bfloat16 [64, 256, 256], P('rows'), as said below
- pattern: int32 [64, 8], P('rows'), may hold values from 0 to 63, as said below
- live_counts: int32 [64], P('rows'), may hold values from 0 to 8, as said below
Outputs:
- solution: bfloat16 [16384, 512], P('rows', 'rhs')
Inputs may be any that keep to these rules, and one draw needn't show every extreme that they name: pattern[s, k] names a block row of a lower level than s; slot 0 of every block row above level 0 names a block row of the level just below; rows of level 0 hold 0. Block row t is held by index t // 8 of rows; the used slots of the block rows held by one index of rows name, for any one level, at most 2 distinct block rows held by any one other index. `live_counts`: 0 on level 0, from 1 to 8 on higher levels, 8 reached. `diag_inverse`: each block is the inverse of a well-conditioned diagonal block of the factor.
All inputs are finite; a program needn't handle non-finite values.
Results may differ from a plain program's by a relative error of at most 0.0058.
Values may be sent and summed in bfloat16 or wider, within the bound.
A program may use at most 128 MiB of HBM per device.

v0:
```python
import jax
import jax.numpy as jnp
from jax import lax
from jax.sharding import PartitionSpec as P

LEV = 4


def shards(kernel_rows, factor_blocks, diag_inverse, pattern, live_counts):
    received = lax.all_to_all(kernel_rows, "rhs", split_axis=1, concat_axis=0, tiled=True)
    per_device = factor_blocks.shape[0]
    slot_count = factor_blocks.shape[1]
    block = factor_blocks.shape[2]
    width = received.shape[1]
    right_side = received.reshape(per_device, block, width)
    holders = lax.axis_size("rows")
    per_level = per_device // LEV
    level_size = holders * per_level
    level_of = pattern % per_device // per_level
    holder_of = pattern // per_device
    offset_of = pattern % per_level
    active = jnp.arange(slot_count)[None, :] < live_counts[:, None]
    position = holder_of * per_level + offset_of
    flat_index = level_of * level_size + position
    gathered_all = []
    solved_all = []
    for level_now in range(LEV):
        lower = level_now * per_level
        upper = lower + per_level
        if level_now == 0:
            summed_now = jnp.zeros((per_level, block, width), jnp.float32)
        else:
            available = jnp.concatenate(gathered_all, axis=0)
            picked = jnp.take(available, flat_index[lower:upper], axis=0, mode="clip")
            picked = jnp.where(active[lower:upper, :, None, None], picked, jnp.zeros_like(picked))
            summed_now = jnp.einsum(
                "bkij,bkjr->bir",
                factor_blocks[lower:upper],
                picked,
                preferred_element_type=jnp.float32,
            )
        residual = (right_side[lower:upper].astype(jnp.float32) - summed_now).astype(jnp.bfloat16)
        solved = jnp.einsum(
            "bij,bjr->bir", diag_inverse[lower:upper], residual, preferred_element_type=jnp.float32
        ).astype(jnp.bfloat16)
        solved_all.append(solved)
        if level_now + 1 < LEV:
            incoming = lax.all_gather(solved, "rows", axis=0, tiled=True)
            gathered_all.append(incoming)
    return jnp.concatenate(solved_all, axis=0).reshape(per_device * block, width)


def solution(mesh):
    placed = (
        P(("rows", "rhs"), None),
        P("rows", None, None, None),
        P("rows", None, None),
        P("rows", None),
        P("rows"),
    )
    return jax.shard_map(
        shards, mesh=mesh, in_specs=placed, out_specs=P("rows", "rhs"), check_vma=False
    )
```

profile of v0, /device:TPU:2, one launch (start us, length us, event | category | flops | bytes accessed | tf_op | source)
XLA Modules:
  0.0 169.3 jit_solution(5716187824825379785)
XLA Ops:
  6.5 1.3 copy.30
  7.9 10.3 %all_to_all.16 = bf16[512,4,128]{0,2,1:T(8,128)(2,1)S(1)} all-to-all(bf16[512,4,128]{0,2,1:T(8,128)(2,1)S(1)} %bitcast.60), channel_id=1, replica_groups=mesh['rows'=8,'rhs'=4] {'rhs'}, dimensions={1} | all-to-all | bytes 1048576 | tf_op jit(solution)/shard_map/all_to_all | solution.py:10
  18.2 0.1 fusion.84
  18.2 0.1 copy.31
  18.4 0.9 convolution_convert_fusion
  19.3 0.0 all-gather.6.cloned.1.call-start
  19.4 0.1 reshape.28
  19.5 0.1 iota_compare_fusion
  19.6 0.1 copy.32
  19.7 0.1 copy.34
  19.8 41.2 %all-gather.4.cloned.1.call-done = bf16[16,256,128]{2,1,0:T(8,128)(2,1)} async-done(((bf16[2,256,128]{2,1,0:T(8,128)(2,1)}), bf16[16,256,128]{2,1,0:T(8,128)(2,1)}) %all-gather.4.cloned.1.call-update) | async-done | bytes 1048592 | tf_op jit(solution)/shard_map/all_gather | solution.py:48
  61.0 2.0 %gather_fusion = bf16[16,256,128]{2,1,0:T(8,128)(2,1)S(1)} fusion(bf16[16,256,128]{2,1,0:T(8,128)(2,1)} %all-gather.4.cloned.1.call-done, s32[1024]{0:T(1024)S(1)} %pad_clamp_fusion.2), kind=kCustom, calls=%fused_computation | custom fusion | bytes 2097216 | tf_op jit(solution)/shard_map/jit(_take)/gather | solution.py:34
  63.0 0.5 copy.33
  63.6 3.4 %fusion.39 = bf16[2,256,128]{2,1,0:T(8,128)(2,1)} fusion(f32[2,256,128]{1,2,0:T(8,128)S(1)} %copy.34, bf16[8,8,256,256]{3,2,1,0:T(8,128)(2,1)} %param.6, bf16[2,8,256,128]{2,3,1,0:T(8,128)(2,1)S(1)} %copy.33, pred[2,8]{1,0:T(4,128)(4,1)S(1)} %get-tuple-element.14, bf16[8,256,256]{2,1,0:T(8,128)(2,1)} %param.7), kind=kOutput, calls=%fused_computation.24 | convolution fusion | flops 302710784 | bytes 3801104 | tf_op jit(solution)/shard_map/bij,bjr->bir/dot_general | solution.py:43
  66.9 0.0 all-gather.8.cloned.1.call-start
  67.0 0.1 reshape.36
  67.1 0.1 copy.36
  67.2 0.8 copy.38
  68.1 37.9 %all-gather.6.cloned.1.call-done = bf16[16,256,128]{2,1,0:T(8,128)(2,1)} async-done(((bf16[2,256,128]{2,1,0:T(8,128)(2,1)}), bf16[16,256,128]{2,1,0:T(8,128)(2,1)}) %all-gather.6.cloned.1.call-update) | async-done | bytes 1048592 | tf_op jit(solution)/shard_map/all_gather | solution.py:48
  106.0 1.4 pad_maximum_fusion.1
  107.4 1.7 gather_fusion.1
  109.1 1.5 copy.37
  110.6 3.4 %fusion.42 = bf16[2,256,128]{2,1,0:T(8,128)(2,1)} fusion(f32[2,256,128]{1,2,0:T(8,128)} %copy.38, bf16[8,8,256,256]{3,2,1,0:T(8,128)(2,1)} %param.6, bf16[2,8,256,128]{2,3,1,0:T(8,128)(2,1)S(1)} %copy.37, pred[2,8]{1,0:T(4,128)(4,1)S(1)} %get-tuple-element.13, bf16[8,256,256]{2,1,0:T(8,128)(2,1)} %param.7), kind=kOutput, calls=%fused_computation.25 | convolution fusion | flops 302710784 | bytes 3801104 | tf_op jit(solution)/shard_map/bij,bjr->bir/dot_general | solution.py:43
  114.0 0.1 reshape.44
  114.1 0.1 copy.40
  114.2 0.1 copy.42
  114.4 38.7 %all-gather.8.cloned.1.call-done = bf16[16,256,128]{2,1,0:T(8,128)(2,1)} async-done(((bf16[2,256,128]{2,1,0:T(8,128)(2,1)}), bf16[16,256,128]{2,1,0:T(8,128)(2,1)}) %all-gather.8.cloned.1.call-update) | async-done | bytes 1048592 | tf_op jit(solution)/shard_map/all_gather | solution.py:48
  153.1 2.9 %pad_maximum_fusion = bf16[48,256,128]{2,1,0:T(8,128)(2,1)} fusion(bf16[16,256,128]{2,1,0:T(8,128)(2,1)} %all-gather.8.cloned.1.call-done, bf16[16,256,128]{2,1,0:T(8,128)(2,1)S(1)} %copy-done.1, bf16[16,256,128]{2,1,0:T(8,128)(2,1)S(1)} %copy-done), kind=kLoop, calls=%fused_computation.3 | loop fusion | flops 3145728 | bytes 6291456 | tf_op jit(solution)/shard_map/concatenate | solution.py:33
  156.0 2.6 %gather_fusion.2 = bf16[16,256,128]{2,1,0:T(8,128)(2,1)S(1)} fusion(bf16[48,256,128]{2,1,0:T(8,128)(2,1)} %pad_maximum_fusion, s32[1024]{0:T(1024)S(1)} %pad_clamp_fusion), kind=kCustom, calls=%fused_computation.2 | custom fusion | bytes 2097216 | tf_op jit(solution)/shard_map/jit(_take)/gather | solution.py:34
  158.6 0.5 copy.41
  159.2 2.7 %fusion.45 = bf16[2,256,128]{2,1,0:T(8,128)(2,1)S(1)} fusion(f32[2,256,128]{1,2,0:T(8,128)S(1)} %copy.42, bf16[8,8,256,256]{3,2,1,0:T(8,128)(2,1)} %param.6, bf16[2,8,256,128]{2,3,1,0:T(8,128)(2,1)S(1)} %copy.41, pred[2,8]{1,0:T(4,128)(4,1)S(1)} %get-tuple-element.12, bf16[8,256,256]{2,1,0:T(8,128)(2,1)} %param.7), kind=kOutput, calls=%fused_computation.26 | convolution fusion | flops 302710784 | bytes 3801104 | tf_op jit(solution)/shard_map/bij,bjr->bir/dot_general | solution.py:43
  161.9 0.9 pad_maximum_fusion.2
  (26 shorter events, 0.1 us)
Async XLA Ops:
  6.5 11.8 %copy-start.5 = (bf16[8,256,256]{2,1,0:T(8,128)(2,1)S(1)}, bf16[8,256,256]{2,1,0:T(8,128)(2,1)}, u32[]{:S(2)}) copy-start(bf16[8,256,256]{2,1,0:T(8,128)(2,1)} %param.7) | copy-start | bytes 3145732
  6.5 12.8 %copy-start.6 = (s32[8,8]{1,0:T(8,128)S(1)}, s32[8,8]{1,0:T(8,128)}, u32[]{:S(2)}) copy-start(s32[8,8]{1,0:T(8,128)} %param.8) | copy-start | bytes 772
  6.5 12.9 %copy-start.7 = (s32[8]{0:T(128)S(1)}, s32[8]{0:T(128)}, u32[]{:S(2)}) copy-start(s32[8]{0:T(128)} %param.9) | copy-start | bytes 100
  6.5 54.5 %all-gather.4.cloned.1.call-start = ((), (), s32[]{:S(2)}) async-start(), calls=%async_computation.1 | async-start | bytes 1179648 | tf_op jit(solution)/shard_map/all_gather | solution.py:48
  19.3 86.7 %all-gather.6.cloned.1.call-start = ((), (), s32[]{:S(2)}) async-start(), calls=%async_computation.2 | async-start | bytes 1179648 | tf_op jit(solution)/shard_map/all_gather | solution.py:48
  63.5 42.5 %copy-start = (bf16[16,256,128]{2,1,0:T(8,128)(2,1)S(1)}, bf16[16,256,128]{2,1,0:T(8,128)(2,1)}, u32[]{:S(2)}) copy-start(bf16[16,256,128]{2,1,0:T(8,128)(2,1)} %all-gather.4.cloned.1.call-done) | copy-start | bytes 3145732
  66.9 86.1 %all-gather.8.cloned.1.call-start = ((), (), s32[]{:S(2)}) async-start(), calls=%async_computation.3 | async-start | bytes 1179648 | tf_op jit(solution)/shard_map/all_gather | solution.py:48
  110.6 42.5 %copy-start.1 = (bf16[16,256,128]{2,1,0:T(8,128)(2,1)S(1)}, bf16[16,256,128]{2,1,0:T(8,128)(2,1)}, u32[]{:S(2)}) copy-start(bf16[16,256,128]{2,1,0:T(8,128)(2,1)} %all-gather.6.cloned.1.call-done) | copy-start | bytes 3145732
  159.1 2.7 %copy-start.2 = (bf16[2,256,128]{2,1,0:T(8,128)(2,1)S(1)}, bf16[2,256,128]{2,1,0:T(8,128)(2,1)}, u32[]{:S(2)}) copy-start(bf16[2,256,128]{2,1,0:T(8,128)(2,1)} %convolution_convert_fusion) | copy-start | bytes 393220
  159.1 2.7 %copy-start.3 = (bf16[2,256,128]{2,1,0:T(8,128)(2,1)S(1)}, bf16[2,256,128]{2,1,0:T(8,128)(2,1)}, u32[]{:S(2)}) copy-start(bf16[2,256,128]{2,1,0:T(8,128)(2,1)} %fusion.39) | copy-start | bytes 393220
  159.2 2.7 %copy-start.4 = (bf16[2,256,128]{2,1,0:T(8,128)(2,1)S(1)}, bf16[2,256,128]{2,1,0:T(8,128)(2,1)}, u32[]{:S(2)}) copy-start(bf16[2,256,128]{2,1,0:T(8,128)(2,1)} %fusion.42) | copy-start | bytes 393220
Sparse Core Ops, SparseCore 0:
  19.4 41.5 all-gather.3
  67.1 38.8 all-gather.5
  114.1 38.8 all-gather.7
where the time goes:
time: 171 us; the launch traced here: 169 us
  waiting for transfers between devices  118 us (69%)
  between operations  13.3 us (8%)
  local copies, waits for them, and re-layouts  12 us (7%)
  blocking collectives  10.3 us (6%)
  matrix products  10.3 us (6%)
  other arithmetic  5.32 us (3%)
    all_gather x3, waiting for transfers between devices, shards(): incoming = lax.all_gather(solved, 'rows', axis=0, tiled=True)  118 us
    dot_general x4, matrix products, shards(): jnp.einsum('bij,bjr->bir', diag_inverse[lower:upper], residual, preferred...  10.3 us
    all_to_all x1, blocking collectives, shards(): lax.all_to_all(kernel_rows, 'rhs', split_axis=1, concat_axis=0, tiled=True)  10.3 us
    gather x6, local copies, waits for them, and re-layouts, shards(): picked = jnp.take(available, flat_index[lower:upper], axis=0, mode='clip')  8.82 us
    concatenate x2, other arithmetic, shards(): available = jnp.concatenate(gathered_all, axis=0)  4.27 us
  transfers between devices with their start and end apart: 3, of which 3 were waited for; matrix products, arithmetic and copies ran while one was open for 1% of the time, Pallas kernels for 0%

commit v1 on v0

v1 whole, which is shorter than its diff:
```python
import functools

import jax
import jax.numpy as jnp
from jax import lax
from jax.experimental import pallas as pl
from jax.experimental.pallas import tpu as pltpu
from jax.sharding import PartitionSpec as P

LEV = 4
MESH = pl.DeviceIdType.MESH


def kernel(rows, rhs, kr_hbm, fb_hbm, di_hbm, pat, live, out,
           right, factor, inverse, *rest):
    held = rest[: LEV - 1]
    fb_sem, di_sem, own_sem, kr_send, kr_recv, x_send, x_recv = rest[LEV - 1 :]
    per_device, slots, block, _ = fb_hbm.shape
    per_level = per_device // LEV
    width = out.shape[1]
    part = kr_hbm.shape[0]
    outer = rows // 2
    me_r = lax.axis_index("rows")
    me_h = lax.axis_index("rhs")
    z, y = me_r // 2, me_r % 2
    across = z * 2 + (1 - y)

    def line(d):
        return lax.rem(z + d, outer) * 2 + y

    fb_copies = []
    for lev in range(1, LEV):
        at = pl.ds(lev * per_level, per_level)
        fb_copies.append(pltpu.make_async_copy(
            fb_hbm.at[at], factor.at[pl.ds((lev - 1) * per_level, per_level)], fb_sem.at[lev - 1]))
    di_copy = pltpu.make_async_copy(di_hbm, inverse, di_sem)
    mine = pl.ds(pl.multiple_of(me_h * part, part), part)
    own_copy = pltpu.make_async_copy(
        kr_hbm.at[:, pl.ds(pl.multiple_of(me_h * width, width), width)], right.at[mine], own_sem)
    own_copy.start()
    di_copy.start()
    for c in fb_copies:
        c.start()

    barrier = pltpu.get_barrier_semaphore()
    for d in range(1, outer):
        pl.semaphore_signal(barrier, inc=1, device_id=(line(d), me_h), device_id_type=MESH)
    pl.semaphore_signal(barrier, inc=1, device_id=(across, me_h), device_id_type=MESH)
    for d in range(1, rhs):
        pl.semaphore_signal(barrier, inc=1, device_id=(me_r, lax.rem(me_h + d, rhs)), device_id_type=MESH)
    pl.semaphore_wait(barrier, outer - 1 + 1 + rhs - 1)

    kr_copies = []
    for d in range(1, rhs):
        peer = lax.rem(me_h + d, rhs)
        c = pltpu.make_async_remote_copy(
            src_ref=kr_hbm.at[:, pl.ds(pl.multiple_of(peer * width, width), width)],
            dst_ref=right.at[mine],
            send_sem=kr_send.at[d - 1], recv_sem=kr_recv.at[d - 1],
            device_id=(me_r, peer), device_id_type=MESH)
        c.start()
        kr_copies.append(c)

    def wait_rows(sender):
        @pl.when(me_h == sender)
        def _():
            own_copy.wait()

        for d in range(1, rhs):
            @pl.when(lax.rem(sender + d, rhs) == me_h)
            def _(d=d):
                kr_copies[d - 1].wait_recv()

    def send(lev, o, j, owner, target):
        ref = held[lev].at[owner, o]
        c = pltpu.make_async_remote_copy(
            src_ref=ref, dst_ref=ref,
            send_sem=x_send.at[lev, o, j], recv_sem=x_recv.at[lev, o, j],
            device_id=(target, me_h), device_id_type=MESH)
        c.start()
        return c

    started = []
    waited = 0
    near = sorted(range(1, outer), key=lambda d: min(d, outer - d))
    di_copy.wait()
    for lev in range(LEV):
        top = (lev + 1) * per_level * block
        while waited < rhs and waited * part < top:
            wait_rows(waited)
            waited += 1
        if lev:
            fb_copies[lev - 1].wait()
        direct = {}
        for o in range(per_level):
            s = lev * per_level + o
            at = pl.ds(s * block, block)
            residual = right[at]
            if lev:
                total = jnp.zeros((block, width), jnp.float32)
                for k in range(slots):
                    name = pat[s, k]
                    holder = name // per_device
                    local = name % per_device
                    of_level = local // per_level
                    offset = local % per_level
                    x = held[0][holder, offset]
                    for l in range(1, lev):
                        x = jnp.where(of_level == l, held[l][holder, offset], x)
                    x = jnp.where(k < live[s], x, jnp.zeros_like(x))
                    total += jnp.dot(factor[s - per_level, k], x, preferred_element_type=jnp.float32)
                residual = (residual.astype(jnp.float32) - total).astype(jnp.bfloat16)
            solved = jnp.dot(inverse[s], residual, preferred_element_type=jnp.float32).astype(jnp.bfloat16)
            out[at] = solved
            if lev + 1 < LEV:
                held[lev][me_r, o] = solved
                for d in near:
                    direct[o, d] = send(lev, o, d - 1, me_r, line(d))
                direct[o, 0] = send(lev, o, outer - 1, me_r, across)
        if lev + 1 < LEV:
            passed = []
            for d in near:
                for o in range(per_level):
                    direct[o, d].wait_recv()
                    passed.append(send(lev, o, outer - 1 + d, line(outer - d), across))
            for o in range(per_level):
                direct[o, 0].wait_recv()
            for c in passed:
                c.wait_recv()
            started += list(direct.values()) + passed
    for c in kr_copies + started:
        c.wait_send()


def shards(rows, rhs, kernel_rows, factor_blocks, diag_inverse, pattern, live_counts):
    per_device, slots, block, _ = factor_blocks.shape
    per_level = per_device // LEV
    width = kernel_rows.shape[1] // rhs
    kinds = 2 * (rows // 2) - 1
    bf = jnp.bfloat16
    any_spec = pl.BlockSpec(memory_space=pl.ANY)
    smem = pl.BlockSpec(memory_space=pltpu.SMEM)
    dma = pltpu.SemaphoreType.DMA
    return pl.pallas_call(
        functools.partial(kernel, rows, rhs),
        out_shape=jax.ShapeDtypeStruct((per_device * block, width), bf),
        in_specs=[any_spec, any_spec, any_spec, smem, smem],
        out_specs=pl.BlockSpec(memory_space=pltpu.VMEM),
        scratch_shapes=[
            pltpu.VMEM((per_device * block, width), bf),
            pltpu.VMEM((per_device - per_level, slots, block, block), bf),
            pltpu.VMEM((per_device, block, block), bf),
            *[pltpu.VMEM((rows, per_level, block, width), bf) for _ in range(LEV - 1)],
            dma((LEV - 1,)),
            dma,
            dma,
            dma((rhs - 1,)),
            dma((rhs - 1,)),
            dma((LEV - 1, per_level, kinds)),
            dma((LEV - 1, per_level, kinds)),
        ],
        compiler_params=pltpu.CompilerParams(
            collective_id=0, has_side_effects=True, vmem_limit_bytes=56 * 1024 * 1024
        ),
        cost_estimate=pl.CostEstimate(
            flops=2 * per_device * (slots + 1) * block * block * width,
            bytes_accessed=2 * per_device * slots * block * block,
            transcendentals=0,
        ),
    )(kernel_rows, factor_blocks, diag_inverse, pattern, live_counts)


def solution(mesh):
    placed = (
        P(("rows", "rhs"), None),
        P("rows", None, None, None),
        P("rows", None, None),
        P("rows", None),
        P("rows"),
    )
    body = functools.partial(shards, mesh.shape["rows"], mesh.shape["rhs"])
    return jax.shard_map(
        body, mesh=mesh, in_specs=placed, out_specs=P("rows", "rhs"), check_vma=False
    )
```

time: 171 us -> 69 us (0.40)
  the two profiles are of different devices: /device:TPU:2 before, /device:TPU:19 now
where the time goes in v1:
time: 69 us; the launch traced here: 68.8 us
  Pallas kernels  66.9 us (97%)
  local copies, waits for them, and re-layouts  1.87 us (3%)
    pallas_call x1, Pallas kernels, shards(): pl.pallas_call(functools.partial(kernel, rows, rhs), out_shape=jax.ShapeD...  66.9 us
    unnamed x1, local copies, waits for them, and re-layouts  1.87 us

profile of v1, /device:TPU:19, one launch (start us, length us, event | category | flops | bytes accessed | tf_op | source)
XLA Modules:
  0.0 68.8 jit_solution(8774846137224396417)
XLA Ops:
  0.0 66.9 %shard_map.55 = bf16[2048,128]{1,0:T(8,128)(2,1)} custom-call(bf16[512,512]{1,0:T(8,128)(2,1)} %kr_hbm.1, bf16[8,8,256,256]{3,2,1,0:T(8,128)(2,1)} %fb_hbm.1, bf16[8,256,256]{2,1,0:T(8,128)(2,1)} %di_hbm.1, s32[8,8]{1,0:T(8,128)} %pat.1, s32[8]{0:T(128)} %live.1), custom_call_target="tpu_custom_call" | custom-call | flops 1207959552 | bytes 8388608 | tf_op jit(solution)/shard_map/pallas_call | solution.py:144
  67.0 1.9 %copy.7 = bf16[2048,128]{1,0:T(8,128)(2,1)} copy(bf16[2048,128]{1,0:T(8,128)(2,1)} %shard_map.55) | data formatting | bytes 1048576

commit v2 on v1

--- a/solution.py
+++ b/solution.py
@@ -25,9 +25,6 @@
     z, y = me_r // 2, me_r % 2
     across = z * 2 + (1 - y)
 
-    def line(d):
-        return lax.rem(z + d, outer) * 2 + y
-
     fb_copies = []
     for lev in range(1, LEV):
         at = pl.ds(lev * per_level, per_level)
@@ -43,12 +40,13 @@
         c.start()
 
     barrier = pltpu.get_barrier_semaphore()
-    for d in range(1, outer):
-        pl.semaphore_signal(barrier, inc=1, device_id=(line(d), me_h), device_id_type=MESH)
+    for d in (1, outer - 1):
+        near = lax.rem(z + d, outer) * 2 + y
+        pl.semaphore_signal(barrier, inc=1, device_id=(near, me_h), device_id_type=MESH)
     pl.semaphore_signal(barrier, inc=1, device_id=(across, me_h), device_id_type=MESH)
     for d in range(1, rhs):
         pl.semaphore_signal(barrier, inc=1, device_id=(me_r, lax.rem(me_h + d, rhs)), device_id_type=MESH)
-    pl.semaphore_wait(barrier, outer - 1 + 1 + rhs - 1)
+    pl.semaphore_wait(barrier, 2 + 1 + rhs - 1)
 
     kr_copies = []
     for d in range(1, rhs):
@@ -58,8 +56,12 @@
             dst_ref=right.at[mine],
             send_sem=kr_send.at[d - 1], recv_sem=kr_recv.at[d - 1],
             device_id=(me_r, peer), device_id_type=MESH)
-        c.start()
         kr_copies.append(c)
+
+    @pl.when(me_h == 0)
+    def _():
+        for c in kr_copies:
+            c.start()
 
     def wait_rows(sender):
         @pl.when(me_h == sender)
@@ -71,27 +73,40 @@
             def _(d=d):
                 kr_copies[d - 1].wait_recv()
 
-    def send(lev, o, j, owner, target):
-        ref = held[lev].at[owner, o]
-        c = pltpu.make_async_remote_copy(
+    def copy(lev, o, owner, side, sent, landed, target):
+        ref = held[lev].at[owner * 2 + side, o]
+        return pltpu.make_async_remote_copy(
             src_ref=ref, dst_ref=ref,
-            send_sem=x_send.at[lev, o, j], recv_sem=x_recv.at[lev, o, j],
+            send_sem=x_send.at[lev, o, sent], recv_sem=x_recv.at[lev, o, landed],
             device_id=(target, me_h), device_id_type=MESH)
-        c.start()
-        return c
-
-    started = []
+
+    def up(lev, o, owner):
+        return copy(lev, o, owner, y, owner, owner, me_r + 2)
+
+    def down(lev, o, owner):
+        return copy(lev, o, owner, y, owner + 1, owner, me_r - 2)
+
+    def over(lev, o, owner):
+        return copy(lev, o, owner, y, outer + 1 + owner, outer + owner, across)
+
+    def from_over(lev, o, owner):
+        return copy(lev, o, owner, 1 - y, outer + 1 + owner, outer + owner, across)
+
+    below, above = z > 0, z < outer - 1
     waited = 0
-    near = sorted(range(1, outer), key=lambda d: min(d, outer - d))
     di_copy.wait()
     for lev in range(LEV):
         top = (lev + 1) * per_level * block
         while waited < rhs and waited * part < top:
             wait_rows(waited)
+            if waited == 0:
+                @pl.when(me_h != 0)
+                def _():
+                    for c in kr_copies:
+                        c.start()
             waited += 1
         if lev:
             fb_copies[lev - 1].wait()
-        direct = {}
         for o in range(per_level):
             s = lev * per_level + o
             at = pl.ds(s * block, block)
@@ -114,29 +129,62 @@
             out[at] = solved
             if lev + 1 < LEV:
                 held[lev][me_r, o] = solved
-                for d in near:
-                    direct[o, d] = send(lev, o, d - 1, me_r, line(d))
-                direct[o, 0] = send(lev, o, outer - 1, me_r, across)
+
+                @pl.when(above)
+                def _(o=o):
+                    up(lev, o, z).start()
+
+                @pl.when(below)
+                def _(o=o):
+                    down(lev, o, z).start()
+
+                over(lev, o, z).start()
         if lev + 1 < LEV:
-            passed = []
-            for d in near:
+            for t in range(1, outer):
                 for o in range(per_level):
-                    direct[o, d].wait_recv()
-                    passed.append(send(lev, o, outer - 1 + d, line(outer - d), across))
-            for o in range(per_level):
-                direct[o, 0].wait_recv()
-            for c in passed:
-                c.wait_recv()
-            started += list(direct.values()) + passed
-    for c in kr_copies + started:
+                    @pl.when(z >= t)
+                    def _(o=o, t=t):
+                        up(lev, o, z - t).wait_recv()
+
+                        @pl.when(above)
+                        def _():
+                            up(lev, o, z - t).start()
+
+                        over(lev, o, z - t).start()
+
+                    @pl.when(z + t < outer)
+                    def _(o=o, t=t):
+                        down(lev, o, z + t).wait_recv()
+
+                        @pl.when(below)
+                        def _():
+                            down(lev, o, z + t).start()
+
+                        over(lev, o, z + t).start()
+            for owner in range(outer):
+                for o in range(per_level):
+                    from_over(lev, o, owner).wait_recv()
+    for c in kr_copies:
         c.wait_send()
+    for lev in range(LEV - 1):
+        for o in range(per_level):
+            for t in range(outer):
+                @pl.when((z >= t) & above)
+                def _(lev=lev, o=o, t=t):
+                    up(lev, o, z - t).wait_send()
+
+                @pl.when((z + t < outer) & below)
+                def _(lev=lev, o=o, t=t):
+                    down(lev, o, z + t).wait_send()
+
+                over(lev, o, t).wait_send()
 
 
 def shards(rows, rhs, kernel_rows, factor_blocks, diag_inverse, pattern, live_counts):
     per_device, slots, block, _ = factor_blocks.shape
     per_level = per_device // LEV
     width = kernel_rows.shape[1] // rhs
-    kinds = 2 * (rows // 2) - 1
+    outer = rows // 2
     bf = jnp.bfloat16
     any_spec = pl.BlockSpec(memory_space=pl.ANY)
     smem = pl.BlockSpec(memory_space=pltpu.SMEM)
@@ -156,8 +204,8 @@
             dma,
             dma((rhs - 1,)),
             dma((rhs - 1,)),
-            dma((LEV - 1, per_level, kinds)),
-            dma((LEV - 1, per_level, kinds)),
+            dma((LEV - 1, per_level, 2 * outer + 1)),
+            dma((LEV - 1, per_level, 2 * outer)),
         ],
         compiler_params=pltpu.CompilerParams(
             collective_id=0, has_side_effects=True, vmem_limit_bytes=56 * 1024 * 1024

time: 69 us -> 58.9 us (0.85)
  the two profiles are of different devices: /device:TPU:19 before, /device:TPU:2 now
where the time goes in v2:
time: 58.9 us; the launch traced here: 58.7 us
  Pallas kernels  56.9 us (97%)
  local copies, waits for them, and re-layouts  1.87 us (3%)
    pallas_call x1, Pallas kernels, shards(): pl.pallas_call(functools.partial(kernel, rows, rhs), out_shape=jax.ShapeD...  56.9 us
    unnamed x1, local copies, waits for them, and re-layouts  1.87 us

profile of v2, /device:TPU:2, one launch (start us, length us, event | category | flops | bytes accessed | tf_op | source)
XLA Modules:
  0.0 58.7 jit_solution(13598070570984763627)
XLA Ops:
  0.0 56.9 %shard_map.55 = bf16[2048,128]{1,0:T(8,128)(2,1)} custom-call(bf16[512,512]{1,0:T(8,128)(2,1)} %kr_hbm.1, bf16[8,8,256,256]{3,2,1,0:T(8,128)(2,1)} %fb_hbm.1, bf16[8,256,256]{2,1,0:T(8,128)(2,1)} %di_hbm.1, s32[8,8]{1,0:T(8,128)} %pat.1, s32[8]{0:T(128)} %live.1), custom_call_target="tpu_custom_call" | custom-call | flops 1207959552 | bytes 8388608 | tf_op jit(solution)/shard_map/pallas_call | solution.py:192
  56.9 1.9 %copy.7 = bf16[2048,128]{1,0:T(8,128)(2,1)} copy(bf16[2048,128]{1,0:T(8,128)(2,1)} %shard_map.55) | data formatting | bytes 1048576

commit v3 on v2

--- a/solution.py
+++ b/solution.py
@@ -73,24 +73,33 @@
             def _(d=d):
                 kr_copies[d - 1].wait_recv()
 
-    def copy(lev, o, owner, side, sent, landed, target):
-        ref = held[lev].at[owner * 2 + side, o]
+    first = block - block * 3 // 16
+    whole, head, tail = (0, block), (0, first), (first, block - first)
+
+    def copy(lev, o, owner, side, span, sent, landed, target):
+        ref = held[lev].at[owner * 2 + side, o, pl.ds(*span)]
         return pltpu.make_async_remote_copy(
             src_ref=ref, dst_ref=ref,
             send_sem=x_send.at[lev, o, sent], recv_sem=x_recv.at[lev, o, landed],
             device_id=(target, me_h), device_id_type=MESH)
 
     def up(lev, o, owner):
-        return copy(lev, o, owner, y, owner, owner, me_r + 2)
+        return copy(lev, o, owner, y, whole, owner, owner, me_r + 2)
 
     def down(lev, o, owner):
-        return copy(lev, o, owner, y, owner + 1, owner, me_r - 2)
-
-    def over(lev, o, owner):
-        return copy(lev, o, owner, y, outer + 1 + owner, outer + owner, across)
-
-    def from_over(lev, o, owner):
-        return copy(lev, o, owner, 1 - y, outer + 1 + owner, outer + owner, across)
+        return copy(lev, o, owner, y, whole, owner + 1, owner, me_r - 2)
+
+    def up_tail(lev, o, owner):
+        return copy(lev, o, owner, 1 - y, tail, 2 * outer + 1 + owner, 2 * outer + owner, me_r + 2)
+
+    def down_tail(lev, o, owner):
+        return copy(lev, o, owner, 1 - y, tail, 2 * outer + 2 + owner, 2 * outer + owner, me_r - 2)
+
+    def over(lev, o, owner, span=head):
+        return copy(lev, o, owner, y, span, outer + 1 + owner, outer + owner, across)
+
+    def from_over(lev, o, owner, span=head):
+        return copy(lev, o, owner, 1 - y, span, outer + 1 + owner, outer + owner, across)
 
     below, above = z > 0, z < outer - 1
     waited = 0
@@ -138,7 +147,7 @@
                 def _(o=o):
                     down(lev, o, z).start()
 
-                over(lev, o, z).start()
+                over(lev, o, z, whole).start()
         if lev + 1 < LEV:
             for t in range(1, outer):
                 for o in range(per_level):
@@ -161,9 +170,36 @@
                             down(lev, o, z + t).start()
 
                         over(lev, o, z + t).start()
-            for owner in range(outer):
-                for o in range(per_level):
-                    from_over(lev, o, owner).wait_recv()
+                for o in range(per_level):
+                    if t == 1:
+                        from_over(lev, o, z, whole).wait_recv()
+
+                        @pl.when(above)
+                        def _(o=o):
+                            up_tail(lev, o, z).start()
+
+                        @pl.when(below)
+                        def _(o=o):
+                            down_tail(lev, o, z).start()
+                for o in range(per_level):
+                    @pl.when(z >= t)
+                    def _(o=o, t=t):
+                        up_tail(lev, o, z - t).wait_recv()
+
+                        @pl.when(above)
+                        def _():
+                            up_tail(lev, o, z - t).start()
+
+                    @pl.when(z + t < outer)
+                    def _(o=o, t=t):
+                        down_tail(lev, o, z + t).wait_recv()
+
+                        @pl.when(below)
+                        def _():
+                            down_tail(lev, o, z + t).start()
+            for t in range(1, outer):
+                for o in range(per_level):
+                    from_over(lev, o, lax.rem(z + t, outer)).wait_recv()
     for c in kr_copies:
         c.wait_send()
     for lev in range(LEV - 1):
@@ -172,12 +208,14 @@
                 @pl.when((z >= t) & above)
                 def _(lev=lev, o=o, t=t):
                     up(lev, o, z - t).wait_send()
+                    up_tail(lev, o, z - t).wait_send()
 
                 @pl.when((z + t < outer) & below)
                 def _(lev=lev, o=o, t=t):
                     down(lev, o, z + t).wait_send()
-
-                over(lev, o, t).wait_send()
+                    down_tail(lev, o, z + t).wait_send()
+
+                over(lev, o, lax.rem(z + t, outer), head if t else whole).wait_send()
 
 
 def shards(rows, rhs, kernel_rows, factor_blocks, diag_inverse, pattern, live_counts):
@@ -204,8 +242,8 @@
             dma,
             dma((rhs - 1,)),
             dma((rhs - 1,)),
-            dma((LEV - 1, per_level, 2 * outer + 1)),
-            dma((LEV - 1, per_level, 2 * outer)),
+            dma((LEV - 1, per_level, 3 * outer + 2)),
+            dma((LEV - 1, per_level, 3 * outer)),
         ],
         compiler_params=pltpu.CompilerParams(
             collective_id=0, has_side_effects=True, vmem_limit_bytes=56 * 1024 * 1024

time: 58.9 us -> 64.3 us (1.092)
  Pallas kernels: 56.9 us -> 62.2 us
    pallas_call x1, Pallas kernels: 56.9 us -> 62.2 us  [shards(): pl.pallas_call(functools.partial(kernel, rows, rhs), out_shape=jax.ShapeD...]
where the time goes in v3:
time: 64.3 us; the launch traced here: 64.1 us
  Pallas kernels  62.2 us (97%)
  local copies, waits for them, and re-layouts  1.87 us (3%)
    pallas_call x1, Pallas kernels, shards(): pl.pallas_call(functools.partial(kernel, rows, rhs), out_shape=jax.ShapeD...  62.2 us
    unnamed x1, local copies, waits for them, and re-layouts  1.87 us

profile of v3, /device:TPU:2, one launch (start us, length us, event | category | flops | bytes accessed | tf_op | source)
XLA Modules:
  0.0 64.1 jit_solution(4023980358856835321)
XLA Ops:
  0.0 62.2 %shard_map.55 = bf16[2048,128]{1,0:T(8,128)(2,1)} custom-call(bf16[512,512]{1,0:T(8,128)(2,1)} %kr_hbm.1, bf16[8,8,256,256]{3,2,1,0:T(8,128)(2,1)} %fb_hbm.1, bf16[8,256,256]{2,1,0:T(8,128)(2,1)} %di_hbm.1, s32[8,8]{1,0:T(8,128)} %pat.1, s32[8]{0:T(128)} %live.1), custom_call_target="tpu_custom_call" | custom-call | flops 1207959552 | bytes 8388608 | tf_op jit(solution)/shard_map/pallas_call | solution.py:230
  62.3 1.9 %copy.7 = bf16[2048,128]{1,0:T(8,128)(2,1)} copy(bf16[2048,128]{1,0:T(8,128)(2,1)} %shard_map.55) | data formatting | bytes 1048576

commit v4 on v2

--- a/solution.py
+++ b/solution.py
@@ -73,8 +73,11 @@
             def _(d=d):
                 kr_copies[d - 1].wait_recv()
 
+    sub = 2
+    share = block // sub
+
     def copy(lev, o, owner, side, sent, landed, target):
-        ref = held[lev].at[owner * 2 + side, o]
+        ref = held[lev].at[owner * 2 + side, o // sub, pl.ds(o % sub * share, share)]
         return pltpu.make_async_remote_copy(
             src_ref=ref, dst_ref=ref,
             send_sem=x_send.at[lev, o, sent], recv_sem=x_recv.at[lev, o, landed],
@@ -130,18 +133,19 @@
             if lev + 1 < LEV:
                 held[lev][me_r, o] = solved
 
-                @pl.when(above)
-                def _(o=o):
-                    up(lev, o, z).start()
-
-                @pl.when(below)
-                def _(o=o):
-                    down(lev, o, z).start()
-
-                over(lev, o, z).start()
+                for o in range(o * sub, (o + 1) * sub):
+                    @pl.when(above)
+                    def _(o=o):
+                        up(lev, o, z).start()
+
+                    @pl.when(below)
+                    def _(o=o):
+                        down(lev, o, z).start()
+
+                    over(lev, o, z).start()
         if lev + 1 < LEV:
             for t in range(1, outer):
-                for o in range(per_level):
+                for o in range(per_level * sub):
                     @pl.when(z >= t)
                     def _(o=o, t=t):
                         up(lev, o, z - t).wait_recv()
@@ -162,12 +166,12 @@
 
                         over(lev, o, z + t).start()
             for owner in range(outer):
-                for o in range(per_level):
+                for o in range(per_level * sub):
                     from_over(lev, o, owner).wait_recv()
     for c in kr_copies:
         c.wait_send()
     for lev in range(LEV - 1):
-        for o in range(per_level):
+        for o in range(per_level * sub):
             for t in range(outer):
                 @pl.when((z >= t) & above)
                 def _(lev=lev, o=o, t=t):
@@ -204,8 +208,8 @@
             dma,
             dma((rhs - 1,)),
             dma((rhs - 1,)),
-            dma((LEV - 1, per_level, 2 * outer + 1)),
-            dma((LEV - 1, per_level, 2 * outer)),
+            dma((LEV - 1, per_level * 2, 2 * outer + 1)),
+            dma((LEV - 1, per_level * 2, 2 * outer)),
         ],
         compiler_params=pltpu.CompilerParams(
             collective_id=0, has_side_effects=True, vmem_limit_bytes=56 * 1024 * 1024

time: 58.9 us -> 56.9 us (0.966)
  Pallas kernels: 56.9 us -> 54.8 us
    pallas_call x1, Pallas kernels: 56.9 us -> 54.8 us  [shards(): pl.pallas_call(functools.partial(kernel, rows, rhs), out_shape=jax.ShapeD...]
where the time goes in v4:
time: 56.9 us; the launch traced here: 56.7 us
  Pallas kernels  54.8 us (96%)
  local copies, waits for them, and re-layouts  1.87 us (3%)
    pallas_call x1, Pallas kernels, shards(): pl.pallas_call(functools.partial(kernel, rows, rhs), out_shape=jax.ShapeD...  54.8 us
    unnamed x1, local copies, waits for them, and re-layouts  1.87 us

profile of v4, /device:TPU:2, one launch (start us, length us, event | category | flops | bytes accessed | tf_op | source)
XLA Modules:
  0.0 56.7 jit_solution(15948022033632404897)
XLA Ops:
  0.0 54.8 %shard_map.55 = bf16[2048,128]{1,0:T(8,128)(2,1)} custom-call(bf16[512,512]{1,0:T(8,128)(2,1)} %kr_hbm.1, bf16[8,8,256,256]{3,2,1,0:T(8,128)(2,1)} %fb_hbm.1, bf16[8,256,256]{2,1,0:T(8,128)(2,1)} %di_hbm.1, s32[8,8]{1,0:T(8,128)} %pat.1, s32[8]{0:T(128)} %live.1), custom_call_target="tpu_custom_call" | custom-call | flops 1207959552 | bytes 8388608 | tf_op jit(solution)/shard_map/pallas_call | solution.py:196
  54.8 1.9 %copy.7 = bf16[2048,128]{1,0:T(8,128)(2,1)} copy(bf16[2048,128]{1,0:T(8,128)(2,1)} %shard_map.55) | data formatting | bytes 1048576
